TPU v7x, 32 devices: a whole 2x2x4 slice. The times are simulated.
32 devices in a mesh: dp: 8 (over y, x, core), mp: 4 (over z).
Axes of the slice: x: 2, y: 2, z: 4, core: 2. Of those that a mesh axis runs over, the one named last changes fastest.
Arguments:
- frames: bfloat16 [11008, 768], P(('dp', 'mp')), may hold values from -6 to 6
- span_mask: int32 [16, 688], P('dp'), may hold values from 0 to 1, as said below
- cotangent: bfloat16 [11008, 768], P(('dp', 'mp')), may hold values from -6 to 6
- qkv_weight: float32 [768, 2304], P('dp', 'mp'), may hold values from -0.21875 to 0.21875
- qkv_mean: float32 [768, 2304], P('dp', 'mp'), may hold values from -0.00061035156 to 0.00061035156
- qkv_square: float32 [768, 2304], P('dp', 'mp'), may hold values from 7.064254e-11 to 1.1302806e-09
- out_weight: float32 [768, 768], P('mp', 'dp'), may hold values from -3.5 to 3.5
- out_mean: float32 [768, 768], P('mp', 'dp'), may hold values from -0.00061035156 to 0.00061035156
- out_square: float32 [768, 768], P('mp', 'dp'), may hold values from 2.8257017e-12 to 4.2385526e-11
- up_weight: float32 [768, 3072], P('dp', 'mp'), may hold values from -0.21875 to 0.21875
- up_mean: float32 [768, 3072], P('dp', 'mp'), may hold values from -0.00061035156 to 0.00061035156
- up_square: float32 [768, 3072], P('dp', 'mp'), may hold values from 7.064254e-11 to 1.1302806e-09
- down_weight: float32 [3072, 768], P('mp', 'dp'), may hold values from -0.109375 to 0.109375
- down_mean: float32 [3072, 768], P('mp', 'dp'), may hold values from -0.00061035156 to 0.00061035156
- down_square: float32 [3072, 768], P('mp', 'dp'), may hold values from 7.064254e-11 to 1.1302806e-09
- head_biases: float32 [12, 384], P('mp', 'dp'), may hold values from -4 to 4
- bias_mean: float32 [12, 384], P('mp', 'dp'), may hold values from -0.00061035156 to 0.00061035156
- bias_square: float32 [12, 384], P('mp', 'dp'), may hold values from 7.064254e-11 to 1.1302806e-09
- norm_vectors: float32 [7, 768], P(None, 'dp'), may hold values from -4 to 4
- vector_mean: float32 [7, 768], P(None, 'dp'), may hold values from -0.00061035156 to 0.00061035156
- vector_square: float32 [7, 768], P(None, 'dp'), may hold values from 7.064254e-11 to 1.1302806e-09
Outputs:
- activations: float32 [11008, 768], P(('dp', 'mp'))
- frame_grad: float32 [11008, 768], P(('dp', 'mp'))
- grad_norm: float32 [], replicated
- qkv_master: float32 [768, 2304], P('dp', 'mp')
- qkv_moment: float32 [768, 2304], P('dp', 'mp')
- qkv_variance: float32 [768, 2304], P('dp', 'mp')
- out_master: float32 [768, 768], P('mp', 'dp')
- out_moment: float32 [768, 768], P('mp', 'dp')
- out_variance: float32 [768, 768], P('mp', 'dp')
- up_master: float32 [768, 3072], P('dp', 'mp')
- up_moment: float32 [768, 3072], P('dp', 'mp')
- up_variance: float32 [768, 3072], P('dp', 'mp')
- down_master: float32 [3072, 768], P('mp', 'dp')
- down_moment: float32 [3072, 768], P('mp', 'dp')
- down_variance: float32 [3072, 768], P('mp', 'dp')
- bias_master: float32 [12, 384], P('mp', 'dp')
- bias_moment: float32 [12, 384], P('mp', 'dp')
- bias_variance: float32 [12, 384], P('mp', 'dp')
- vector_master: float32 [7, 768], P(None, 'dp')
- vector_moment: float32 [7, 768], P(None, 'dp')
- vector_variance: float32 [7, 768], P(None, 'dp')
Inputs may be any that keep to these rules, and one draw needn't show every extreme that they name: `span_mask`: masked frames come in spans of 10 consecutive frames begun at random frames of a clip (spans may join or be cut by the clip's end); the share of masked frames differs from clip to clip.
All inputs are finite; a program needn't handle non-finite values.
Results may differ from a plain program's by a relative error of at most 0.017.
Values may be sent and summed in bfloat16 or wider, within the bound.
A program may use at most 128 MiB of HBM per device.

v0:
```python
import jax
import jax.numpy as jnp
from jax import lax
from jax.sharding import PartitionSpec as P

HD = 64
LEN = 688
norm_eps = 1e-05
adam_eps = 1e-08
beta_one = 0.9
beta_two = 0.999
step_count = 10.0
clip_limit = 1.0
settings = ((0.05, 0.1), (0.3, 0.1), (0.05, 0.1), (0.03, 0.1), (0.3, 0.0), (0.4, 0.0))


def norm_rows(values, norm_gain, norm_shift):
    centred = values - jnp.mean(values, axis=-1, keepdims=True)
    variance = jnp.mean(centred * centred, axis=-1, keepdims=True)
    inverse = lax.rsqrt(variance + norm_eps)
    normed = centred * inverse
    return (normed * norm_gain + norm_shift, normed, inverse)


def norm_back(upstream, normed, inverse, norm_gain):
    scaled = upstream * norm_gain
    inner_part = (
        scaled
        - jnp.mean(scaled, axis=-1, keepdims=True)
        - normed * jnp.mean(scaled * normed, axis=-1, keepdims=True)
    )
    return (inverse * inner_part, jnp.sum(upstream * normed, axis=0), jnp.sum(upstream, axis=0))


def gelu_slope(pre_act):
    cumulative = 0.5 * (1.0 + jax.scipy.special.erf(pre_act * 0.7071067811865476))
    return cumulative + pre_act * jnp.exp(-0.5 * pre_act * pre_act) * 0.3989422804014327


def attend_forward(clip_block):
    scaling = HD ** (-0.5)
    queries = clip_block[:, :, 0]
    key_rows = clip_block[:, :, 1]
    value_rows = clip_block[:, :, 2]
    scores = (
        jnp.einsum("qhe,khe->hqk", queries, key_rows, preferred_element_type=jnp.float32) * scaling
    )
    row_peak = jnp.max(scores, axis=-1, keepdims=True)
    log_total = row_peak + jnp.log(jnp.sum(jnp.exp(scores - row_peak), axis=-1, keepdims=True))
    attention = jnp.exp(scores - log_total).astype(jnp.bfloat16)
    mixed_rows = jnp.einsum(
        "hqk,khe->qhe", attention, value_rows, preferred_element_type=jnp.float32
    )
    return (mixed_rows.astype(jnp.bfloat16).reshape(clip_block.shape[0], -1), log_total)


def attend_backward(pieces):
    clip_block, log_total, grad_mixed = pieces
    scaling = HD ** (-0.5)
    queries = clip_block[:, :, 0]
    key_rows = clip_block[:, :, 1]
    value_rows = clip_block[:, :, 2]
    scores = (
        jnp.einsum("qhe,khe->hqk", queries, key_rows, preferred_element_type=jnp.float32) * scaling
    )
    attention = jnp.exp(scores - log_total)
    attention_low = attention.astype(jnp.bfloat16)
    mixed_rows = jnp.einsum(
        "hqk,khe->qhe", attention_low, value_rows, preferred_element_type=jnp.float32
    ).astype(jnp.bfloat16)
    grad_rows = grad_mixed.reshape(queries.shape)
    grad_attention = jnp.einsum(
        "qhe,khe->hqk", grad_rows, value_rows, preferred_element_type=jnp.float32
    )
    grad_values = jnp.einsum(
        "hqk,qhe->khe", attention_low, grad_rows, preferred_element_type=jnp.float32
    )
    row_inner = jnp.sum(attention * grad_attention, axis=-1, keepdims=True)
    grad_scores = (attention * (grad_attention - row_inner)).astype(jnp.bfloat16)
    grad_queries = (
        jnp.einsum("hqk,khe->qhe", grad_scores, key_rows, preferred_element_type=jnp.float32)
        * scaling
    )
    grad_keys = (
        jnp.einsum("hqk,qhe->khe", grad_scores, queries, preferred_element_type=jnp.float32)
        * scaling
    )
    grad_block = jnp.stack([grad_queries, grad_keys, grad_values], axis=2).astype(jnp.bfloat16)
    return (
        mixed_rows.reshape(clip_block.shape[0], -1),
        grad_block.reshape(clip_block.shape[0], -1),
    )


def adam_step(weight, mean_old, square_old, gradient, factor, rate, decay):
    clipped = gradient * factor
    mean_new = beta_one * mean_old + (1.0 - beta_one) * clipped
    square_new = beta_two * square_old + (1.0 - beta_two) * clipped * clipped
    mean_hat = mean_new / (1.0 - beta_one**step_count)
    square_hat = square_new / (1.0 - beta_two**step_count)
    weight_new = weight - rate * (mean_hat / (jnp.sqrt(square_hat) + adam_eps) + decay * weight)
    return (weight_new, mean_new, square_new)


def on_device(
    frames,
    span_mask,
    cotangent,
    qkv_weight,
    qkv_mean,
    qkv_square,
    out_weight,
    out_mean,
    out_square,
    up_weight,
    up_mean,
    up_square,
    down_weight,
    down_mean,
    down_square,
    head_biases,
    bias_mean,
    bias_square,
    norm_vectors,
    vector_mean,
    vector_square,
):
    masters = (qkv_weight, out_weight, up_weight, down_weight, head_biases, norm_vectors)
    lowered = tuple((weight.astype(jnp.bfloat16) for weight in masters))
    qkv_full, out_full, up_full, down_full, bias_full, vector_full = (
        lax.all_gather(lowered[0], "dp", axis=0, tiled=True),
        lax.all_gather(lowered[1], "dp", axis=1, tiled=True),
        lax.all_gather(lowered[2], "dp", axis=0, tiled=True),
        lax.all_gather(lowered[3], "dp", axis=1, tiled=True),
        lax.all_gather(lowered[4], "dp", axis=1, tiled=True),
        lax.all_gather(lowered[5], "dp", axis=1, tiled=True),
    )
    share_rows = frames.shape[0]
    start_row = lax.axis_index("mp") * share_rows
    vectors = vector_full.astype(jnp.float32)
    local_heads = bias_full.shape[0]

    def share_of(array_full):
        return lax.dynamic_slice_in_dim(array_full, start_row, share_rows, 0)

    gathered = lax.all_gather(frames, "mp", axis=0, tiled=True)
    all_rows = gathered.shape[0]
    masked = span_mask.reshape(all_rows, 1) == 1
    inputs = jnp.where(masked, vectors[0], gathered.astype(jnp.float32))
    rounded = inputs.astype(jnp.bfloat16)
    zero_bias = jnp.zeros_like(bias_full[:, :HD])
    qkv_bias = (
        jnp.stack([bias_full[:, :HD], zero_bias, bias_full[:, HD : 2 * HD]], axis=1)
        .reshape(-1)
        .astype(jnp.float32)
    )
    up_bias = bias_full[:, 2 * HD :].reshape(-1).astype(jnp.float32)
    projected = (jnp.dot(rounded, qkv_full, preferred_element_type=jnp.float32) + qkv_bias).astype(
        jnp.bfloat16
    )
    blocks = projected.reshape(-1, LEN, local_heads, 3, HD)
    mixed_rows, log_total = lax.map(attend_forward, blocks)
    mixed_rows = mixed_rows.reshape(all_rows, -1)
    attn_part = jnp.dot(mixed_rows, out_full, preferred_element_type=jnp.float32)
    attended = lax.psum(attn_part, "mp")
    first_sum = inputs + attended + vectors[5]
    hidden, normed_full, inverse_full = norm_rows(first_sum, vectors[1], vectors[2])
    normed_one = share_of(normed_full)
    inverse_one = share_of(inverse_full)
    hidden_low = hidden.astype(jnp.bfloat16)
    pre_act = jnp.dot(hidden_low, up_full, preferred_element_type=jnp.float32) + up_bias
    activated = jax.nn.gelu(pre_act, approximate=False).astype(jnp.bfloat16)
    ffn_part = jnp.dot(activated, down_full, preferred_element_type=jnp.float32)
    second_sum = hidden + lax.psum(ffn_part, "mp") + vectors[6]
    outputs_full, normed_full, inverse_full = norm_rows(second_sum, vectors[3], vectors[4])
    outputs = share_of(outputs_full)
    normed_two = share_of(normed_full)
    inverse_two = share_of(inverse_full)
    qkv_full, out_full, up_full, down_full, bias_full, vector_full = (
        lax.all_gather(lowered[0], "dp", axis=0, tiled=True),
        lax.all_gather(lowered[1], "dp", axis=1, tiled=True),
        lax.all_gather(lowered[2], "dp", axis=0, tiled=True),
        lax.all_gather(lowered[3], "dp", axis=1, tiled=True),
        lax.all_gather(lowered[4], "dp", axis=1, tiled=True),
        lax.all_gather(lowered[5], "dp", axis=1, tiled=True),
    )
    upstream = cotangent.astype(jnp.float32)
    grad_two, grad_gain_two, grad_shift_two = norm_back(
        upstream, normed_two, inverse_two, vectors[3]
    )
    grad_down_bias = jnp.sum(grad_two, axis=0)
    grad_two_full = lax.all_gather(grad_two.astype(jnp.bfloat16), "mp", axis=0, tiled=True)
    pre_again = jnp.dot(hidden_low, up_full, preferred_element_type=jnp.float32) + up_bias
    act_again = jax.nn.gelu(pre_again, approximate=False).astype(jnp.bfloat16)
    grad_down = jnp.einsum(
        "tf,td->fd", act_again, grad_two_full, preferred_element_type=jnp.float32
    )
    grad_act = jnp.einsum("td,fd->tf", grad_two_full, down_full, preferred_element_type=jnp.float32)
    grad_pre = (grad_act * gelu_slope(pre_again)).astype(jnp.bfloat16)
    grad_up = jnp.einsum("td,tf->df", hidden_low, grad_pre, preferred_element_type=jnp.float32)
    grad_up_bias = jnp.sum(grad_pre, axis=0, dtype=jnp.float32)
    hidden_part = jnp.einsum("tf,df->td", grad_pre, up_full, preferred_element_type=jnp.float32)
    grad_hidden = grad_two + lax.psum_scatter(hidden_part, "mp", scatter_dimension=0, tiled=True)
    grad_one, grad_gain_one, grad_shift_one = norm_back(
        grad_hidden, normed_one, inverse_one, vectors[1]
    )
    grad_out_bias = jnp.sum(grad_one, axis=0)
    grad_one_full = lax.all_gather(grad_one.astype(jnp.bfloat16), "mp", axis=0, tiled=True)
    grad_mixed = jnp.einsum(
        "td,cd->tc", grad_one_full, out_full, preferred_element_type=jnp.float32
    ).astype(jnp.bfloat16)
    mixed_again, grad_blocks = lax.map(
        attend_backward, (blocks, log_total, grad_mixed.reshape(-1, LEN, grad_mixed.shape[1]))
    )
    mixed_again = mixed_again.reshape(all_rows, -1)
    grad_blocks = grad_blocks.reshape(all_rows, -1)
    grad_out = jnp.einsum(
        "tc,td->cd", mixed_again, grad_one_full, preferred_element_type=jnp.float32
    )
    grad_qkv = jnp.einsum("td,tc->dc", rounded, grad_blocks, preferred_element_type=jnp.float32)
    bias_sums = jnp.sum(grad_blocks, axis=0, dtype=jnp.float32).reshape(local_heads, 3, HD)
    grad_biases = jnp.concatenate(
        [bias_sums[:, 0], bias_sums[:, 2], grad_up_bias.reshape(local_heads, -1)], axis=1
    )
    input_part = jnp.einsum("tc,dc->td", grad_blocks, qkv_full, preferred_element_type=jnp.float32)
    grad_inputs = grad_one + lax.psum_scatter(
        input_part.astype(jnp.bfloat16), "mp", scatter_dimension=0, tiled=True
    ).astype(jnp.float32)
    masked_share = share_of(masked)
    grad_embed = jnp.sum(jnp.where(masked_share, grad_inputs, 0.0), axis=0)
    frame_grad = jnp.where(masked_share, 0.0, grad_inputs)
    grad_vectors = jnp.stack(
        [
            grad_embed,
            grad_gain_one,
            grad_shift_one,
            grad_gain_two,
            grad_shift_two,
            grad_out_bias,
            grad_down_bias,
        ]
    )
    reduced = (
        lax.psum_scatter(grad_qkv, "dp", scatter_dimension=0, tiled=True),
        lax.psum_scatter(grad_out, "dp", scatter_dimension=1, tiled=True),
        lax.psum_scatter(grad_up, "dp", scatter_dimension=0, tiled=True),
        lax.psum_scatter(grad_down, "dp", scatter_dimension=1, tiled=True),
        lax.psum_scatter(grad_biases, "dp", scatter_dimension=1, tiled=True),
    )
    local_squares = jnp.float32(0.0)
    for portion in reduced:
        local_squares = local_squares + jnp.sum(portion * portion)
    total_squares, vector_total = lax.psum((local_squares, grad_vectors), ("dp", "mp"))
    grad_norm = jnp.sqrt(total_squares + jnp.sum(vector_total * vector_total))
    column_count = norm_vectors.shape[1]
    vector_grad = lax.dynamic_slice_in_dim(
        vector_total, lax.axis_index("dp") * column_count, column_count, 1
    )
    factor = jnp.minimum(1.0, clip_limit / (grad_norm + 1e-06))
    gradients = (reduced[0], reduced[1], reduced[2], reduced[3], reduced[4], vector_grad)
    means = (qkv_mean, out_mean, up_mean, down_mean, bias_mean, vector_mean)
    squares = (qkv_square, out_square, up_square, down_square, bias_square, vector_square)
    updated = []
    for index_at in range(6):
        updated.extend(
            adam_step(
                masters[index_at],
                means[index_at],
                squares[index_at],
                gradients[index_at],
                factor,
                settings[index_at][0],
                settings[index_at][1],
            )
        )
    return (
        outputs,
        frame_grad,
        grad_norm,
        updated[0],
        updated[1],
        updated[2],
        updated[3],
        updated[4],
        updated[5],
        updated[6],
        updated[7],
        updated[8],
        updated[9],
        updated[10],
        updated[11],
        updated[12],
        updated[13],
        updated[14],
        updated[15],
        updated[16],
        updated[17],
    )


def solution(mesh):
    return jax.shard_map(
        on_device,
        mesh=mesh,
        in_specs=(
            P(("dp", "mp"), None),
            P("dp", None),
            P(("dp", "mp"), None),
            P("dp", "mp"),
            P("dp", "mp"),
            P("dp", "mp"),
            P("mp", "dp"),
            P("mp", "dp"),
            P("mp", "dp"),
            P("dp", "mp"),
            P("dp", "mp"),
            P("dp", "mp"),
            P("mp", "dp"),
            P("mp", "dp"),
            P("mp", "dp"),
            P("mp", "dp"),
            P("mp", "dp"),
            P("mp", "dp"),
            P(None, "dp"),
            P(None, "dp"),
            P(None, "dp"),
        ),
        out_specs=(
            P(("dp", "mp"), None),
            P(("dp", "mp"), None),
            P(),
            P("dp", "mp"),
            P("dp", "mp"),
            P("dp", "mp"),
            P("mp", "dp"),
            P("mp", "dp"),
            P("mp", "dp"),
            P("dp", "mp"),
            P("dp", "mp"),
            P("dp", "mp"),
            P("mp", "dp"),
            P("mp", "dp"),
            P("mp", "dp"),
            P("mp", "dp"),
            P("mp", "dp"),
            P("mp", "dp"),
            P(None, "dp"),
            P(None, "dp"),
            P(None, "dp"),
        ),
        check_vma=False,
    )
```

profile of v0, /device:TPU:0, one launch (start us, length us, event | category | flops | bytes accessed | tf_op | source)
XLA Modules:
  0.0 884.5 jit_solution(6685718186284344518)
XLA Ops:
  10.3 10.3 %all-gather.1 = bf16[8,48,3]{1,2,0:T(4,128)(2,1)S(1)} all-gather(bf16[1,48,3]{1,2,0:T(4,128)(2,1)S(1)} %convert_bitcast_fusion.1), channel_id=1, replica_groups=mesh['dp'=8,'mp'=4] {'dp'}, dimensions={0}, use_global_device_ids=true | all-gather | bytes 2592 | tf_op jit(solution)/shard_map/all_gather | solution.py:135
  22.2 8.9 %all-gather = bf16[8,96,7]{1,2,0:T(8,128)(2,1)S(1)} all-gather(bf16[1,96,7]{1,2,0:T(8,128)(2,1)S(1)} %convert_bitcast_fusion), channel_id=1, replica_groups=mesh['dp'=8,'mp'=4] {'dp'}, dimensions={0}, use_global_device_ids=true | all-gather | bytes 12096 | tf_op jit(solution)/shard_map/all_gather | solution.py:136
  33.1 9.6 %all_gather.35 = bf16[192,768]{0,1:T(8,128)(2,1)} all-gather(bf16[192,96]{0,1:T(8,128)(2,1)S(1)} %copy.106), channel_id=1, replica_groups=mesh['dp'=8,'mp'=4] {'dp'}, dimensions={1}, use_global_device_ids=true | all-gather | bytes 331776 | tf_op jit(solution)/shard_map/all_gather | solution.py:132
  43.4 11.0 %all_gather.33 = bf16[768,576]{1,0:T(8,128)(2,1)S(1)} all-gather(bf16[96,576]{1,0:T(8,128)(2,1)S(1)} %convert_element_type.121), channel_id=1, replica_groups=mesh['dp'=8,'mp'=4] {'dp'}, dimensions={0}, use_global_device_ids=true | all-gather | bytes 995328 | tf_op jit(solution)/shard_map/all_gather | solution.py:131
  54.4 4.8 all-gather.8.cloned.1.call-done
  59.2 3.3 fusion.36
  62.5 2.1 reshape.215
  65.0 7.0 while.24
  66.1 1.1 exponential_reduce_fusion.2
  67.3 1.1 fusion.110
  69.6 1.1 exponential_reduce_fusion.2
  70.8 1.1 fusion.110
  71.9 1.4 copy.105
  73.4 2.1 reshape.216
  75.5 2.8 fusion.71
  80.9 152.6 %all-reduce.4.cloned.1.call-done = f32[1376,768]{1,0:T(8,128)} async-done(((f32[1376,768]{1,0:T(8,128)}), f32[1376,768]{1,0:T(8,128)}) %all-reduce.4.cloned.1.call-update) | async-done | bytes 4227088 | tf_op jit(solution)/shard_map/psum | solution.py:165
  233.5 4.0 fusion.58
  238.3 1.3 multiply_reduce_fusion.3
  239.6 2.6 subtract_multiply_fusion.1
  242.2 13.6 %fusion.20 = (bf16[1376,768]{1,0:T(8,128)(2,1)}, f32[1376,768]{1,0:T(8,128)}) fusion(f32[768]{0:T(1024)S(1)} %reshape.223, bf16[768,768]{1,0:T(8,128)(2,1)} %all-gather.10.cloned.1.call-done, f32[1376,768]{1,0:T(8,128)} %subtract_multiply_fusion.1, f32[768]{0:T(1024)S(1)} %copy-done.41, f32[768]{0:T(1024)S(1)} %get-tuple-element.145), kind=kOutput, calls=%fused_computation.46 | convolution fusion | flops 1696112640 | bytes 11756544 | tf_op jit(solution)/shard_map/dot_general | solution.py:171
  255.8 5.7 fusion.72
  261.6 155.2 %all-reduce.6.cloned.1.call-done = f32[1376,768]{1,0:T(8,128)} async-done(((f32[1376,768]{1,0:T(8,128)}), f32[1376,768]{1,0:T(8,128)}) %all-reduce.6.cloned.1.call-update) | async-done | bytes 4227088 | tf_op jit(solution)/shard_map/psum | solution.py:174
  416.8 4.3 fusion.69
  423.2 1.3 fusion.66
  425.7 45.2 %all-gather.14.cloned.1.call-done = bf16[1376,768]{1,0:T(8,128)(2,1)} async-done(((bf16[344,768]{1,0:T(8,128)(2,1)}), bf16[1376,768]{1,0:T(8,128)(2,1)}) %all-gather.14.cloned.1.call-update) | async-done | bytes 2113552 | tf_op jit(solution)/shard_map/all_gather | solution.py:192
  470.8 5.2 convert_reduce_fusion
  476.1 1.4 copy-done.48
  477.4 3.9 fusion.73
  481.5 76.0 %reduce-scatter.12.cloned.1.call-done = f32[344,768]{1,0:T(8,128)} async-done(((f32[1376,768]{1,0:T(8,128)}), f32[344,768]{1,0:T(8,128)}) %reduce-scatter.12.cloned.1.call-update) | async-done | bytes 1056784 | tf_op jit(solution)/shard_map/reduce_scatter | solution.py:203
  557.5 2.0 multiply_reduce_fusion.4
  559.5 2.7 fusion.68
  562.3 5.7 fusion.74
  568.1 6.8 fusion.48
  575.3 33.8 %all-gather.16.cloned.1.call-done = bf16[1376,768]{1,0:T(8,128)(2,1)} async-done(((bf16[344,768]{1,0:T(8,128)(2,1)}), bf16[1376,768]{1,0:T(8,128)(2,1)}) %all-gather.16.cloned.1.call-update) | async-done | bytes 2113552 | tf_op jit(solution)/shard_map/all_gather | solution.py:208
  609.2 2.5 convolution_convert_fusion.3
  612.4 21.8 %while.25 = (s32[]{:T(128)}, bf16[2,688,192]{1,2,0:T(8,128)(2,1)S(1)}, bf16[2,688,576]{1,2,0:T(8,128)(2,1)}, bf16[2,688,3,3,64]{1,4,2,3,0:T(8,128)(2,1)S(1)}, f3...) while((s32[]{:T(128)}, bf16[2,688,192]{1,2,0:T(8,128)(2,1)S(1)}, ...), condition=%wide.region_17.18_spmd, body=%wide.region_15.17_spmd.sunk | while | flops 1113468160 | bytes 95243464 | solution.py:212
  613.6 1.1 convolution_convert_fusion.5
  614.8 1.2 fusion.118
  616.0 1.6 multiply_reduce_fusion.16
  617.6 1.5 multiply_convert_fusion.2
  621.3 1.2 copy-done.8
  624.6 1.1 convolution_convert_fusion.5
  625.8 1.2 fusion.118
  627.0 1.6 multiply_reduce_fusion.16
  628.5 1.5 multiply_convert_fusion.2
  632.2 1.2 copy-done.8
  635.3 2.2 convert_reduce_fusion.1
  638.5 3.5 convolution_bitcast_fusion
  642.2 3.9 copy.109
  646.1 5.0 fusion.44
  651.2 4.8 convolution_convert_fusion.2
  656.8 1.7 multiply_reduce_fusion.7
  658.5 1.7 multiply_reduce_fusion.8
  660.3 34.0 %reduce-scatter.24.cloned.1.call-done = f32[48,3]{1,0:T(8,128)} async-done(((f32[384,3]{1,0:T(8,128)}), f32[48,3]{1,0:T(8,128)}) %reduce-scatter.24.cloned.1.call-update) | async-done | bytes 592
  695.7 37.1 %reduce-scatter.22.cloned.1.call-done = f32[96,192]{1,0:T(8,128)} async-done(((f32[768,192]{1,0:T(8,128)}), f32[96,192]{1,0:T(8,128)}) %reduce-scatter.22.cloned.1.call-update) | async-done | bytes 73744
  734.4 42.2 %reduce-scatter.16.cloned.1.call-done = f32[96,576]{1,0:T(8,128)} async-done(((f32[768,576]{1,0:T(8,128)}), f32[96,576]{1,0:T(8,128)}) %reduce-scatter.16.cloned.1.call-update) | async-done | bytes 221200 | tf_op jit(solution)/shard_map/reduce_scatter | solution.py:244
  776.6 1.6 multiply_reduce_fusion.9
  781.5 41.2 %reduce-scatter.14.cloned.1.call-done = bf16[344,768]{1,0:T(8,128)(2,1)} async-done(((bf16[1376,768]{1,0:T(8,128)(2,1)}), bf16[344,768]{1,0:T(8,128)(2,1)}) %reduce-scatter.14.cloned.1.call-update) | async-done | bytes 528400 | tf_op jit(solution)/shard_map/reduce_scatter | solution.py:226
  822.7 2.2 fusion.59
  825.0 40.1 %all-reduce = (f32[]{:T(128)}, f32[7,768]{1,0:T(8,128)S(1)}) all-reduce(f32[]{:T(128)S(6)} %add.297, f32[7,768]{1,0:T(8,128)S(1)} %stack.59), channel_id=1, replica_groups=mesh['dp'=8,'mp'=4] {'dp','mp'}, use_global_device_ids=true, to_apply=%region_31.32 | all-reduce | flops 5377 | bytes 43016 | tf_op jit(solution)/shard_map/psum | solution.py:253
  867.2 1.3 multiply_subtract_fusion.5
  868.5 1.7 multiply_subtract_fusion.3
  870.2 1.4 multiply_subtract_fusion.4
  871.6 2.0 multiply_subtract_fusion.2
  (239 shorter events, 34.8 us)
Async XLA Ops:
  8.0 51.1 %all-gather.8.cloned.1.call-start = ((), (), s32[]{:S(2)}) async-start(), calls=%async_computation.7 | async-start | bytes 2641920 | tf_op jit(solution)/shard_map/all_gather | solution.py:146
  8.8 224.7 %all-reduce.4.cloned.1.call-start = ((), (), s32[]{:S(2)}) async-start(), calls=%async_computation.8 | async-start | bytes 8454144 | tf_op jit(solution)/shard_map/psum | solution.py:165
  9.5 12.6 %copy-start.37 = (pred[2,688]{1,0:T(4,128)(4,1)}, pred[2,688]{1,0:T(4,128)(4,1)S(1)}, u32[]{:S(2)}) copy-start(pred[2,688]{1,0:T(4,128)(4,1)S(1)} %broadcast_compare_fusion) | copy-start | bytes 4132
  9.6 49.5 %copy-start.34 = (pred[1376]{0:T(1024)(128)(4,1)}, pred[1376]{0:T(1024)(128)(4,1)S(1)}, u32[]{:S(2)}) copy-start(pred[1376]{0:T(1024)(128)(4,1)S(1)} %eq.23) | copy-start | bytes 4132
  43.3 196.2 %copy-start.32 = (f32[768]{0:T(1024)}, f32[768]{0:T(1024)S(1)}, u32[]{:S(2)}) copy-start(f32[768]{0:T(1024)S(1)} %get-tuple-element.147) | copy-start | bytes 9220
  54.4 4.8 copy-start.21
  65.0 10.5 %copy-start.10 = (bf16[192,768]{0,1:T(8,128)(2,1)S(1)}, bf16[192,768]{0,1:T(8,128)(2,1)}, u32[]{:S(2)}) copy-start(bf16[192,768]{0,1:T(8,128)(2,1)} %all_gather.35) | copy-start | bytes 884740
  78.3 1.7 copy-start.14
  78.3 2.6 copy-start.40
  78.3 155.2 %copy-start.35 = (pred[1376]{0:T(1024)(128)(4,1)S(1)}, pred[1376]{0:T(1024)(128)(4,1)}, u32[]{:S(2)}) copy-start(pred[1376]{0:T(1024)(128)(4,1)} %copy-done.34) | copy-start | bytes 4132
  78.3 163.9 %all-gather.10.cloned.1.call-start = ((), (), s32[]{:S(2)}) async-start(), calls=%async_computation.9 | async-start | bytes 1327104 | tf_op jit(solution)/shard_map/all_gather | solution.py:133
  79.9 175.9 %all-gather.12.cloned.1.call-start = ((), (), s32[]{:S(2)}) async-start(), calls=%async_computation.10 | async-start | bytes 1327104 | tf_op jit(solution)/shard_map/all_gather | solution.py:134
  80.7 336.1 %all-reduce.6.cloned.1.call-start = ((), (), s32[]{:S(2)}) async-start(), calls=%async_computation.11 | async-start | bytes 8454144 | tf_op jit(solution)/shard_map/psum | solution.py:174
  233.5 4.1 copy-start.2
  233.5 4.8 copy-start.3
  239.6 2.6 copy-start.41
  261.5 155.2 %copy-start.42 = (f32[768]{0:T(1024)S(1)}, f32[768]{0:T(1024)}, u32[]{:S(2)}) copy-start(f32[768]{0:T(1024)} %get-tuple-element.143) | copy-start | bytes 9220
  261.5 209.3 %all-gather.14.cloned.1.call-start = ((), (), s32[]{:S(2)}) async-start(), calls=%async_computation.12 | async-start | bytes 2641920 | tf_op jit(solution)/shard_map/all_gather | solution.py:192
  421.7 1.5 copy-start.44
  425.4 132.1 %reduce-scatter.12.cloned.1.call-start = ((), (), s32[]{:S(2)}) async-start(), calls=%async_computation.13 | async-start | bytes 5283840 | tf_op jit(solution)/shard_map/reduce_scatter | solution.py:203
  470.8 6.6 copy-start.47
  476.1 1.4 copy-start.48
  481.4 127.8 %all-gather.16.cloned.1.call-start = ((), (), s32[]{:S(2)}) async-start(), calls=%async_computation.14 | async-start | bytes 2641920 | tf_op jit(solution)/shard_map/all_gather | solution.py:208
  562.2 94.6 %reduce-scatter.20.cloned.1.call-start = ((), (), s32[]{:S(2)}) async-start(), calls=%async_computation.18 | async-start | bytes 2654208 | tf_op jit(solution)/shard_map/reduce_scatter | solution.py:247
  568.0 90.5 %reduce-scatter.18.cloned.1.call-start = ((), (), s32[]{:S(2)}) async-start(), calls=%async_computation.17 | async-start | bytes 2654208 | tf_op jit(solution)/shard_map/reduce_scatter | solution.py:246
  574.8 37.6 %copy-start.31 = (f32[2,3,688,1]{2,1,3,0:T(4,128)S(1)}, f32[2,3,688,1]{2,1,3,0:T(4,128)}, u32[]{:S(2)}) copy-start(f32[2,3,688,1]{2,1,3,0:T(4,128)} %get-tuple-element.312) | copy-start | bytes 49540
  574.9 119.4 %reduce-scatter.24.cloned.1.call-start = ((), (), s32[]{:S(2)}) async-start(), calls=%async_computation.20 | async-start | bytes 221184
  612.4 2.3 copy-start.5
  612.5 5.1 copy-start
  614.8 2.8 copy-start.11
  619.7 1.5 copy-start.7
  620.7 1.9 copy-start.1
  620.7 2.5 copy-start.6
  620.8 2.7 copy-start.12
  623.5 2.3 copy-start.5
  623.5 5.1 copy-start
  625.8 2.8 copy-start.11
  630.7 1.5 copy-start.7
  631.7 1.7 copy-start.1
  631.7 2.2 copy-start.6
  631.7 2.5 copy-start.12
  637.6 8.5 copy-start.4
  637.6 8.5 copy-start.33
  637.6 8.5 copy-start.36
  638.5 94.3 %reduce-scatter.22.cloned.1.call-start = ((), (), s32[]{:S(2)}) async-start(), calls=%async_computation.19 | async-start | bytes 884736
  642.0 134.6 %reduce-scatter.16.cloned.1.call-start = ((), (), s32[]{:S(2)}) async-start(), calls=%async_computation.16 | async-start | bytes 2211840 | tf_op jit(solution)/shard_map/reduce_scatter | solution.py:244
  646.1 5.1 copy-start.22
  651.1 4.9 copy-start.38
  651.1 171.6 %copy-start.9 = (f32[344,768]{1,0:T(8,128)S(1)}, f32[344,768]{1,0:T(8,128)}, u32[]{:S(2)}) copy-start(f32[344,768]{1,0:T(8,128)} %get-tuple-element.193) | copy-start | bytes 3170308
  651.1 171.6 %reduce-scatter.14.cloned.1.call-start = ((), (), s32[]{:S(2)}) async-start(), calls=%async_computation.15 | async-start | bytes 2641920 | tf_op jit(solution)/shard_map/reduce_scatter | solution.py:226
  656.0 211.2 %copy-start.45 = (f32[3,48]{1,0:T(4,128)S(1)}, f32[3,48]{1,0:T(4,128)}, u32[]{:S(2)}) copy-start(f32[3,48]{1,0:T(4,128)} %param.40) | copy-start | bytes 1732
  656.0 212.5 %copy-start.23 = (f32[192,96]{1,0:T(8,128)S(1)}, f32[192,96]{1,0:T(8,128)}, u32[]{:S(2)}) copy-start(f32[192,96]{1,0:T(8,128)} %param.31) | copy-start | bytes 221188
  656.0 214.2 %copy-start.43 = (f32[7,96]{1,0:T(8,128)S(1)}, f32[7,96]{1,0:T(8,128)}, u32[]{:S(2)}) copy-start(f32[7,96]{1,0:T(8,128)} %param.43) | copy-start | bytes 8068
  656.0 214.2 %copy-start.46 = (f32[7,96]{1,0:T(8,128)S(1)}, f32[7,96]{1,0:T(8,128)}, u32[]{:S(2)}) copy-start(f32[7,96]{1,0:T(8,128)} %param.44) | copy-start | bytes 8068
  656.0 215.6 %copy-start.20 = (f32[96,576]{1,0:T(8,128)S(1)}, f32[96,576]{1,0:T(8,128)}, u32[]{:S(2)}) copy-start(f32[96,576]{1,0:T(8,128)} %param.28) | copy-start | bytes 663556
  656.0 215.6 %copy-start.28 = (f32[96,576]{1,0:T(8,128)S(1)}, f32[96,576]{1,0:T(8,128)}, u32[]{:S(2)}) copy-start(f32[96,576]{1,0:T(8,128)} %param.29) | copy-start | bytes 663556
  656.0 217.6 %copy-start.15 = (f32[768,96]{0,1:T(8,128)S(1)}, f32[768,96]{0,1:T(8,128)}, u32[]{:S(2)}) copy-start(f32[768,96]{0,1:T(8,128)} %param.37) | copy-start | bytes 884740
  656.0 217.6 %copy-start.24 = (f32[768,96]{0,1:T(8,128)S(1)}, f32[768,96]{0,1:T(8,128)}, u32[]{:S(2)}) copy-start(f32[768,96]{0,1:T(8,128)} %param.38) | copy-start | bytes 884740
  656.0 217.6 %copy-start.25 = (f32[768,96]{0,1:T(8,128)S(1)}, f32[768,96]{0,1:T(8,128)}, u32[]{:S(2)}) copy-start(f32[768,96]{0,1:T(8,128)} %param.39) | copy-start | bytes 884740
  656.8 217.9 %copy-start.17 = (f32[96,768]{1,0:T(8,128)S(1)}, f32[96,768]{1,0:T(8,128)}, u32[]{:S(2)}) copy-start(f32[96,768]{1,0:T(8,128)} %param.34) | copy-start | bytes 884740
  656.8 216.8 %copy-start.18 = (f32[768,96]{0,1:T(8,128)S(1)}, f32[768,96]{0,1:T(8,128)}, u32[]{:S(2)}) copy-start(f32[768,96]{0,1:T(8,128)} %reduce-scatter.20.cloned.1.call-done) | copy-start | bytes 884740
  658.5 216.2 %copy-start.19 = (f32[96,768]{1,0:T(8,128)S(1)}, f32[96,768]{1,0:T(8,128)}, u32[]{:S(2)}) copy-start(f32[96,768]{1,0:T(8,128)} %reduce-scatter.18.cloned.1.call-done) | copy-start | bytes 884740
  825.0 49.7 %copy-start.26 = (f32[96,768]{1,0:T(8,128)S(1)}, f32[96,768]{1,0:T(8,128)}, u32[]{:S(2)}) copy-start(f32[96,768]{1,0:T(8,128)} %param.35) | copy-start | bytes 884740
  825.0 49.7 %copy-start.27 = (f32[96,768]{1,0:T(8,128)S(1)}, f32[96,768]{1,0:T(8,128)}, u32[]{:S(2)}) copy-start(f32[96,768]{1,0:T(8,128)} %param.36) | copy-start | bytes 884740
  (9 other events, 9.6 us)
Sparse Core Ops, SparseCore 0:
  10.4 48.6 all-gather.7
  78.4 155.0 all-reduce.3
  261.7 155.0 all-reduce.5
  425.5 45.2 all-gather.13
  481.5 75.9 reduce-scatter.11
  562.3 46.7 all-gather.15
Sparse Core Ops, SparseCore 1:
  81.2 22.9 all-gather.9
  106.5 23.9 all-gather.11
  568.1 42.9 reduce-scatter.19
  614.7 42.4 reduce-scatter.17
  660.8 33.5 reduce-scatter.23
  697.8 34.9 reduce-scatter.21
  736.4 40.1 reduce-scatter.15
  778.8 43.9 reduce-scatter.13
where the time goes:
time: 894 us; the launch traced here: 885 us
  waiting for transfers between devices  623 us (70%)
  matrix products  80.1 us (9%)
  blocking collectives  80 us (9%)
  other arithmetic  50.3 us (6%)
  local copies, waits for them, and re-layouts  26.9 us (3%)
  between operations  22.1 us (2%)
    psum x1, waiting for transfers between devices, on_device(): second_sum = hidden + lax.psum(ffn_part, 'mp') + vectors[6]  155 us
    psum x1, waiting for transfers between devices, on_device(): attended = lax.psum(attn_part, 'mp')  153 us
    reduce_scatter x1, waiting for transfers between devices, on_device(): lax.psum_scatter(hidden_part, 'mp', scatter_dimension=0, tiled=True)  76 us
    unnamed x16, waiting for transfers between devices  72 us
    all_gather x1, waiting for transfers between devices, on_device(): lax.all_gather(grad_two.astype(jnp.bfloat16), 'mp', axis=0, tiled=True)  45.2 us
    reduce_scatter x1, waiting for transfers between devices, on_device(): lax.psum_scatter(grad_qkv, 'dp', scatter_dimension=0, tiled=True)  42.2 us
    reduce_scatter x1, waiting for transfers between devices, on_device(): lax.psum_scatter(input_part.astype(jnp.bfloat16), 'mp', scatter_dimension...  41.2 us
    psum x1, blocking collectives, on_device(): lax.psum((local_squares, grad_vectors), ('dp', 'mp'))  40.1 us
  transfers between devices with their start and end apart: 14, of which 10 were waited for; matrix products, arithmetic and copies ran while one was open for 10% of the time, Pallas kernels for 0%

commit v1 on v0

--- a/solution.py
+++ b/solution.py
@@ -171,7 +171,7 @@
     pre_act = jnp.dot(hidden_low, up_full, preferred_element_type=jnp.float32) + up_bias
     activated = jax.nn.gelu(pre_act, approximate=False).astype(jnp.bfloat16)
     ffn_part = jnp.dot(activated, down_full, preferred_element_type=jnp.float32)
-    second_sum = hidden + lax.psum(ffn_part, "mp") + vectors[6]
+    second_sum = hidden + jnp.sum(lax.all_gather(ffn_part, "mp"), axis=0) + vectors[6]
     outputs_full, normed_full, inverse_full = norm_rows(second_sum, vectors[3], vectors[4])
     outputs = share_of(outputs_full)
     normed_two = share_of(normed_full)

time: 894 us -> 1040 us (1.16)
  waiting for transfers between devices: 623 us -> 756 us
    all_gather x0 -> x1, waiting for transfers between devices: none -> 289 us  [on_device(): lax.all_gather(ffn_part, 'mp')]
    psum x1 -> x0, waiting for transfers between devices: 155 us -> none  [on_device(): second_sum = hidden + lax.psum(ffn_part, 'mp') + vectors[6]]
  transfers between devices with their start and end apart: 14 -> 14, of which waited for: 10 -> 10; matrix products, arithmetic and copies ran while one was open for 10% -> 9% of each run, Pallas kernels for 0% -> 0%
where the time goes in v1:
time: 1040 us; the launch traced here: 1030 us
  waiting for transfers between devices  756 us (73%)
  matrix products  81 us (8%)
  blocking collectives  80 us (8%)
  other arithmetic  59.6 us (6%)
  local copies, waits for them, and re-layouts  28.2 us (3%)
  between operations  22.1 us (2%)
    all_gather x1, waiting for transfers between devices, on_device(): lax.all_gather(ffn_part, 'mp')  289 us
    psum x1, waiting for transfers between devices, on_device(): attended = lax.psum(attn_part, 'mp')  152 us
    reduce_scatter x1, waiting for transfers between devices, on_device(): lax.psum_scatter(hidden_part, 'mp', scatter_dimension=0, tiled=True)  76.1 us
    unnamed x16, waiting for transfers between devices  70.5 us
    all_gather x1, waiting for transfers between devices, on_device(): lax.all_gather(grad_two.astype(jnp.bfloat16), 'mp', axis=0, tiled=True)  45.5 us
    reduce_scatter x1, waiting for transfers between devices, on_device(): lax.psum_scatter(grad_qkv, 'dp', scatter_dimension=0, tiled=True)  42.3 us
    reduce_scatter x1, waiting for transfers between devices, on_device(): lax.psum_scatter(input_part.astype(jnp.bfloat16), 'mp', scatter_dimension...  41.2 us
    psum x1, blocking collectives, on_device(): lax.psum((local_squares, grad_vectors), ('dp', 'mp'))  40.1 us
  transfers between devices with their start and end apart: 14, of which 10 were waited for; matrix products, arithmetic and copies ran while one was open for 9% of the time, Pallas kernels for 0%

profile of v1, /device:TPU:0, one launch (start us, length us, event | category | flops | bytes accessed | tf_op | source)
XLA Modules:
  0.0 1029.1 jit_solution(10268861368586029242)
XLA Ops:
  9.5 10.3 %all-gather.1 = bf16[8,96,7]{1,2,0:T(8,128)(2,1)S(1)} all-gather(bf16[1,96,7]{1,2,0:T(8,128)(2,1)S(1)} %convert_bitcast_fusion), channel_id=1, replica_groups=mesh['dp'=8,'mp'=4] {'dp'}, dimensions={0}, use_global_device_ids=true | all-gather | bytes 12096 | tf_op jit(solution)/shard_map/all_gather | solution.py:136
  21.4 8.9 all-gather.2
  33.1 9.6 all_gather.41
  43.3 11.0 %all_gather.39 = bf16[768,576]{1,0:T(8,128)(2,1)S(1)} all-gather(bf16[96,576]{1,0:T(8,128)(2,1)S(1)} %convert_element_type.121), channel_id=1, replica_groups=mesh['dp'=8,'mp'=4] {'dp'}, dimensions={0}, use_global_device_ids=true | all-gather | bytes 995328 | tf_op jit(solution)/shard_map/all_gather | solution.py:131
  54.4 5.0 all-gather.10.cloned.1.call-done
  59.4 3.4 fusion.36
  62.8 2.1 reshape.215
  65.3 7.0 while.24
  67.6 1.1 fusion.110
  71.0 1.1 fusion.110
  72.2 1.4 copy.105
  73.6 2.1 reshape.216
  75.7 2.8 fusion.71
  81.2 152.3 %all-reduce.3.cloned.1.call-done = f32[1376,768]{1,0:T(8,128)} async-done(((f32[1376,768]{1,0:T(8,128)}), f32[1376,768]{1,0:T(8,128)}) %all-reduce.3.cloned.1.call-update) | async-done | bytes 4227088 | tf_op jit(solution)/shard_map/psum | solution.py:165
  233.5 4.0 fusion.58
  238.3 1.3 multiply_reduce_fusion.3
  239.6 2.6 subtract_multiply_fusion.1
  242.2 13.6 %fusion.20 = (bf16[1376,768]{1,0:T(8,128)(2,1)}, f32[1376,768]{1,0:T(8,128)}) fusion(f32[768]{0:T(1024)S(1)} %reshape.223, bf16[768,768]{1,0:T(8,128)(2,1)} %all-gather.12.cloned.1.call-done, f32[1376,768]{1,0:T(8,128)} %subtract_multiply_fusion.1, f32[768]{0:T(1024)S(1)} %copy-done.39, f32[768]{0:T(1024)S(1)} %get-tuple-element.145), kind=kOutput, calls=%fused_computation.46 | convolution fusion | flops 1696112640 | bytes 11756544 | tf_op jit(solution)/shard_map/dot_general | solution.py:171
  255.8 5.7 fusion.72
  261.8 289.4 %all-gather.20.cloned.1.call-done = f32[5504,768]{1,0:T(8,128)} async-done(((f32[1376,768]{1,0:T(8,128)}), f32[5504,768]{1,0:T(8,128)}) %all-gather.20.cloned.1.call-update) | async-done | bytes 16908304 | tf_op jit(solution)/shard_map/all_gather | solution.py:174
  551.2 9.4 reduce_sum.236
  560.7 4.3 fusion.69
  567.1 1.3 fusion.66
  569.4 45.5 %all-gather.16.cloned.1.call-done = bf16[1376,768]{1,0:T(8,128)(2,1)} async-done(((bf16[344,768]{1,0:T(8,128)(2,1)}), bf16[1376,768]{1,0:T(8,128)(2,1)}) %all-gather.16.cloned.1.call-update) | async-done | bytes 2113552 | tf_op jit(solution)/shard_map/all_gather | solution.py:192
  614.8 5.2 convert_reduce_fusion
  620.1 1.3 copy-done.46
  621.4 3.8 fusion.73
  625.4 76.1 %reduce-scatter.12.cloned.1.call-done = f32[344,768]{1,0:T(8,128)} async-done(((f32[1376,768]{1,0:T(8,128)}), f32[344,768]{1,0:T(8,128)}) %reduce-scatter.12.cloned.1.call-update) | async-done | bytes 1056784 | tf_op jit(solution)/shard_map/reduce_scatter | solution.py:203
  701.5 2.0 multiply_reduce_fusion.4
  703.5 2.7 fusion.68
  706.2 6.4 fusion.48
  712.7 5.9 fusion.74
  719.1 34.0 %all-gather.18.cloned.1.call-done = bf16[1376,768]{1,0:T(8,128)(2,1)} async-done(((bf16[344,768]{1,0:T(8,128)(2,1)}), bf16[1376,768]{1,0:T(8,128)(2,1)}) %all-gather.18.cloned.1.call-update) | async-done | bytes 2113552 | tf_op jit(solution)/shard_map/all_gather | solution.py:208
  753.1 3.3 convolution_convert_fusion.3
  756.4 2.4 reshape.217
  758.9 21.4 %while.25 = (s32[]{:T(128)}, bf16[2,688,192]{1,2,0:T(8,128)(2,1)S(1)}, bf16[2,688,576]{1,2,0:T(8,128)(2,1)}, bf16[2,688,3,3,64]{1,4,2,3,0:T(8,128)(2,1)S(1)}, f3...) while((s32[]{:T(128)}, bf16[2,688,192]{1,2,0:T(8,128)(2,1)S(1)}, ...), condition=%wide.region_17.18_spmd, body=%wide.region_15.17_spmd.sunk | while | flops 1113468160 | bytes 91016328 | solution.py:212
  760.0 1.1 convolution_convert_fusion.5
  761.3 1.6 multiply_reduce_fusion.16
  762.9 1.5 multiply_convert_fusion.2
  766.0 1.2 fusion.118
  767.7 1.2 copy-done.6
  770.8 1.1 convolution_convert_fusion.5
  772.0 1.6 multiply_reduce_fusion.16
  773.6 1.5 multiply_convert_fusion.2
  776.8 1.2 fusion.118
  778.3 1.2 copy-done.6
  780.3 1.9 convert_reduce_fusion.1
  784.3 3.6 convolution_bitcast_fusion
  788.2 3.9 copy.109
  792.1 5.0 fusion.44
  797.2 4.8 convolution_convert_fusion.2
  802.9 1.7 multiply_reduce_fusion.8
  804.6 1.7 multiply_reduce_fusion.7
  806.3 32.6 %reduce-scatter.24.cloned.1.call-done = f32[48,3]{1,0:T(8,128)} async-done(((f32[384,3]{1,0:T(8,128)}), f32[48,3]{1,0:T(8,128)}) %reduce-scatter.24.cloned.1.call-update) | async-done | bytes 592
  840.3 37.1 %reduce-scatter.22.cloned.1.call-done = f32[96,192]{1,0:T(8,128)} async-done(((f32[768,192]{1,0:T(8,128)}), f32[96,192]{1,0:T(8,128)}) %reduce-scatter.22.cloned.1.call-update) | async-done | bytes 73744
  879.0 42.3 %reduce-scatter.16.cloned.1.call-done = f32[96,576]{1,0:T(8,128)} async-done(((f32[768,576]{1,0:T(8,128)}), f32[96,576]{1,0:T(8,128)}) %reduce-scatter.16.cloned.1.call-update) | async-done | bytes 221200 | tf_op jit(solution)/shard_map/reduce_scatter | solution.py:244
  921.2 1.7 multiply_reduce_fusion.9
  926.1 41.2 %reduce-scatter.14.cloned.1.call-done = bf16[344,768]{1,0:T(8,128)(2,1)} async-done(((bf16[1376,768]{1,0:T(8,128)(2,1)}), bf16[344,768]{1,0:T(8,128)(2,1)}) %reduce-scatter.14.cloned.1.call-update) | async-done | bytes 528400 | tf_op jit(solution)/shard_map/reduce_scatter | solution.py:226
  967.3 2.2 fusion.59
  969.6 40.1 %all-reduce = (f32[]{:T(128)}, f32[7,768]{1,0:T(8,128)S(1)}) all-reduce(f32[]{:T(128)S(6)} %add.295, f32[7,768]{1,0:T(8,128)S(1)} %stack.59), channel_id=1, replica_groups=mesh['dp'=8,'mp'=4] {'dp','mp'}, use_global_device_ids=true, to_apply=%region_31.32 | all-reduce | flops 5377 | bytes 43016 | tf_op jit(solution)/shard_map/psum | solution.py:253
  1011.7 1.3 multiply_subtract_fusion.5
  1013.0 1.7 multiply_subtract_fusion.3
  1014.7 1.4 multiply_subtract_fusion.4
  1017.2 2.1 multiply_subtract_fusion.1
  (232 shorter events, 35.8 us)
Async XLA Ops:
  8.0 51.4 %all-gather.10.cloned.1.call-start = ((), (), s32[]{:S(2)}) async-start(), calls=%async_computation.7 | async-start | bytes 2641920 | tf_op jit(solution)/shard_map/all_gather | solution.py:146
  8.8 224.7 %all-reduce.3.cloned.1.call-start = ((), (), s32[]{:S(2)}) async-start(), calls=%async_computation.8 | async-start | bytes 8454144 | tf_op jit(solution)/shard_map/psum | solution.py:165
  20.6 10.4 %copy-start.35 = (pred[2,688]{1,0:T(4,128)(4,1)}, pred[2,688]{1,0:T(4,128)(4,1)S(1)}, u32[]{:S(2)}) copy-start(pred[2,688]{1,0:T(4,128)(4,1)S(1)} %broadcast_compare_fusion) | copy-start | bytes 4132
  20.7 38.7 %copy-start.32 = (pred[1376]{0:T(1024)(128)(4,1)}, pred[1376]{0:T(1024)(128)(4,1)S(1)}, u32[]{:S(2)}) copy-start(pred[1376]{0:T(1024)(128)(4,1)S(1)} %eq.23) | copy-start | bytes 4132
  43.3 196.2 %copy-start.30 = (f32[768]{0:T(1024)}, f32[768]{0:T(1024)S(1)}, u32[]{:S(2)}) copy-start(f32[768]{0:T(1024)S(1)} %get-tuple-element.147) | copy-start | bytes 9220
  54.4 5.0 copy-start.20
  65.3 10.5 %copy-start.8 = (bf16[192,768]{0,1:T(8,128)(2,1)S(1)}, bf16[192,768]{0,1:T(8,128)(2,1)}, u32[]{:S(2)}) copy-start(bf16[192,768]{0,1:T(8,128)(2,1)} %all_gather.41) | copy-start | bytes 884740
  67.5 1.2 copy-start.28
  71.0 1.2 copy-start.28
  78.5 1.7 copy-start.12
  78.5 2.6 copy-start.38
  78.5 155.0 %copy-start.33 = (pred[1376]{0:T(1024)(128)(4,1)S(1)}, pred[1376]{0:T(1024)(128)(4,1)}, u32[]{:S(2)}) copy-start(pred[1376]{0:T(1024)(128)(4,1)} %copy-done.32) | copy-start | bytes 4132
  78.6 163.6 %all-gather.12.cloned.1.call-start = ((), (), s32[]{:S(2)}) async-start(), calls=%async_computation.9 | async-start | bytes 1327104 | tf_op jit(solution)/shard_map/all_gather | solution.py:133
  80.2 175.6 %all-gather.14.cloned.1.call-start = ((), (), s32[]{:S(2)}) async-start(), calls=%async_computation.10 | async-start | bytes 1327104 | tf_op jit(solution)/shard_map/all_gather | solution.py:134
  81.0 470.3 %all-gather.20.cloned.1.call-start = ((), (), s32[]{:S(2)}) async-start(), calls=%async_computation.18 | async-start | bytes 21135360 | tf_op jit(solution)/shard_map/all_gather | solution.py:174
  233.5 4.1 copy-start.2
  233.5 4.8 copy-start.3
  239.6 2.6 copy-start.39
  261.6 353.3 %all-gather.16.cloned.1.call-start = ((), (), s32[]{:S(2)}) async-start(), calls=%async_computation.11 | async-start | bytes 2641920 | tf_op jit(solution)/shard_map/all_gather | solution.py:192
  551.2 9.4 copy-start.40
  565.7 1.5 copy-start.42
  569.3 132.1 %reduce-scatter.12.cloned.1.call-start = ((), (), s32[]{:S(2)}) async-start(), calls=%async_computation.12 | async-start | bytes 5283840 | tf_op jit(solution)/shard_map/reduce_scatter | solution.py:203
  614.8 6.6 copy-start.45
  620.1 1.3 copy-start.46
  625.3 127.8 %all-gather.18.cloned.1.call-start = ((), (), s32[]{:S(2)}) async-start(), calls=%async_computation.13 | async-start | bytes 2641920 | tf_op jit(solution)/shard_map/all_gather | solution.py:208
  706.2 96.7 %reduce-scatter.18.cloned.1.call-start = ((), (), s32[]{:S(2)}) async-start(), calls=%async_computation.16 | async-start | bytes 2654208 | tf_op jit(solution)/shard_map/reduce_scatter | solution.py:246
  712.6 92.0 %reduce-scatter.20.cloned.1.call-start = ((), (), s32[]{:S(2)}) async-start(), calls=%async_computation.17 | async-start | bytes 2654208 | tf_op jit(solution)/shard_map/reduce_scatter | solution.py:247
  718.6 40.3 %copy-start.29 = (f32[2,3,688,1]{2,1,3,0:T(4,128)S(1)}, f32[2,3,688,1]{2,1,3,0:T(4,128)}, u32[]{:S(2)}) copy-start(f32[2,3,688,1]{2,1,3,0:T(4,128)} %get-tuple-element.312) | copy-start | bytes 49540
  718.6 120.2 %reduce-scatter.24.cloned.1.call-start = ((), (), s32[]{:S(2)}) async-start(), calls=%async_computation.20 | async-start | bytes 221184
  758.9 3.9 copy-start
  761.3 1.6 copy-start.9
  766.0 1.6 copy-start.5
  767.2 1.9 copy-start.1
  767.2 2.5 copy-start.10
  767.7 1.2 copy-start.6
  769.7 3.9 copy-start
  772.0 1.6 copy-start.9
  776.8 1.5 copy-start.5
  777.9 1.9 copy-start.1
  777.9 2.3 copy-start.10
  778.3 1.2 copy-start.6
  784.2 7.9 copy-start.4
  784.2 7.9 copy-start.31
  784.2 7.9 copy-start.34
  784.3 93.1 %reduce-scatter.22.cloned.1.call-start = ((), (), s32[]{:S(2)}) async-start(), calls=%async_computation.19 | async-start | bytes 884736
  787.9 133.3 %reduce-scatter.16.cloned.1.call-start = ((), (), s32[]{:S(2)}) async-start(), calls=%async_computation.15 | async-start | bytes 2211840 | tf_op jit(solution)/shard_map/reduce_scatter | solution.py:244
  792.1 5.1 copy-start.21
  797.1 4.9 copy-start.36
  797.2 170.2 %copy-start.7 = (f32[344,768]{1,0:T(8,128)S(1)}, f32[344,768]{1,0:T(8,128)}, u32[]{:S(2)}) copy-start(f32[344,768]{1,0:T(8,128)} %get-tuple-element.193) | copy-start | bytes 3170308
  797.2 170.1 %reduce-scatter.14.cloned.1.call-start = ((), (), s32[]{:S(2)}) async-start(), calls=%async_computation.14 | async-start | bytes 2641920 | tf_op jit(solution)/shard_map/reduce_scatter | solution.py:226
  802.0 209.7 %copy-start.43 = (f32[3,48]{1,0:T(4,128)S(1)}, f32[3,48]{1,0:T(4,128)}, u32[]{:S(2)}) copy-start(f32[3,48]{1,0:T(4,128)} %param.40) | copy-start | bytes 1732
  802.0 211.0 %copy-start.22 = (f32[192,96]{1,0:T(8,128)S(1)}, f32[192,96]{1,0:T(8,128)}, u32[]{:S(2)}) copy-start(f32[192,96]{1,0:T(8,128)} %param.31) | copy-start | bytes 221188
  802.0 212.7 %copy-start.41 = (f32[7,96]{1,0:T(8,128)S(1)}, f32[7,96]{1,0:T(8,128)}, u32[]{:S(2)}) copy-start(f32[7,96]{1,0:T(8,128)} %param.43) | copy-start | bytes 8068
  802.0 212.7 %copy-start.44 = (f32[7,96]{1,0:T(8,128)S(1)}, f32[7,96]{1,0:T(8,128)}, u32[]{:S(2)}) copy-start(f32[7,96]{1,0:T(8,128)} %param.44) | copy-start | bytes 8068
  802.0 214.1 %copy-start.13 = (f32[768,96]{0,1:T(8,128)S(1)}, f32[768,96]{0,1:T(8,128)}, u32[]{:S(2)}) copy-start(f32[768,96]{0,1:T(8,128)} %param.37) | copy-start | bytes 884740
  802.0 214.1 %copy-start.23 = (f32[768,96]{0,1:T(8,128)S(1)}, f32[768,96]{0,1:T(8,128)}, u32[]{:S(2)}) copy-start(f32[768,96]{0,1:T(8,128)} %param.38) | copy-start | bytes 884740
  802.0 214.1 %copy-start.24 = (f32[768,96]{0,1:T(8,128)S(1)}, f32[768,96]{0,1:T(8,128)}, u32[]{:S(2)}) copy-start(f32[768,96]{0,1:T(8,128)} %param.39) | copy-start | bytes 884740
  802.1 215.1 %copy-start.15 = (f32[96,768]{1,0:T(8,128)S(1)}, f32[96,768]{1,0:T(8,128)}, u32[]{:S(2)}) copy-start(f32[96,768]{1,0:T(8,128)} %param.34) | copy-start | bytes 884740
  802.8 214.4 %copy-start.16 = (f32[96,768]{1,0:T(8,128)S(1)}, f32[96,768]{1,0:T(8,128)}, u32[]{:S(2)}) copy-start(f32[96,768]{1,0:T(8,128)} %reduce-scatter.18.cloned.1.call-done) | copy-start | bytes 884740
  804.6 214.8 %copy-start.18 = (f32[96,576]{1,0:T(8,128)S(1)}, f32[96,576]{1,0:T(8,128)}, u32[]{:S(2)}) copy-start(f32[96,576]{1,0:T(8,128)} %param.28) | copy-start | bytes 663556
  804.6 211.6 %copy-start.17 = (f32[768,96]{0,1:T(8,128)S(1)}, f32[768,96]{0,1:T(8,128)}, u32[]{:S(2)}) copy-start(f32[768,96]{0,1:T(8,128)} %reduce-scatter.20.cloned.1.call-done) | copy-start | bytes 884740
  921.2 98.1 %copy-start.19 = (f32[96,576]{1,0:T(8,128)S(1)}, f32[96,576]{1,0:T(8,128)}, u32[]{:S(2)}) copy-start(f32[96,576]{1,0:T(8,128)} %reduce-scatter.16.cloned.1.call-done) | copy-start | bytes 663556
  969.6 49.8 %copy-start.25 = (f32[96,576]{1,0:T(8,128)S(1)}, f32[96,576]{1,0:T(8,128)}, u32[]{:S(2)}) copy-start(f32[96,576]{1,0:T(8,128)} %param.29) | copy-start | bytes 663556
  969.6 49.8 %copy-start.26 = (f32[96,576]{1,0:T(8,128)S(1)}, f32[96,576]{1,0:T(8,128)}, u32[]{:S(2)}) copy-start(f32[96,576]{1,0:T(8,128)} %param.30) | copy-start | bytes 663556
  (5 other events, 4.8 us)
Sparse Core Ops, SparseCore 0:
  10.4 48.9 all-gather.9
  78.7 154.7 all-reduce.2
  261.7 289.4 all-gather.19
  569.5 45.3 all-gather.15
  625.4 76.0 reduce-scatter.11
  706.3 46.7 all-gather.17
Sparse Core Ops, SparseCore 1:
  81.5 22.6 all-gather.11
  106.5 23.9 all-gather.13
  712.7 42.8 reduce-scatter.17
  759.3 42.3 reduce-scatter.19
  805.3 33.6 reduce-scatter.23
  842.3 34.9 reduce-scatter.21
  881.0 40.2 reduce-scatter.15
  923.4 43.9 reduce-scatter.13
